TPU v7x, 256 devices: a whole 4x4x8 slice. The times are simulated.
256 devices in a mesh: row: 16 (over x, y), col: 16 (over z, core).
Axes of the slice: x: 4, y: 4, z: 8, core: 2. Of those that a mesh axis runs over, the one named last changes fastest.
Arguments:
- src_points: float32 [73728, 64], P('row'), may hold values from -1.2 to 1.2
- dst_points: float32 [73728, 64], P(('col', 'row')), may hold values from -1.2 to 1.2
- dst_potential: float32 [73728], P(('col', 'row')), may hold values from -1.2 to 25.3
- partners: int32 [288, 28], P('row'), may hold values from 0 to 287, as said below
- partner_count: int32 [288], P('row'), may hold values from 14 to 28
- src_count: int32 [288], P('row'), may hold values from 64 to 256
- dst_count: int32 [288], P('col'), may hold values from 64 to 256
Outputs:
- src_potential: float32 [73728], P('row')
- dst_new: float32 [73728], P(('col', 'row'))
Inputs may be any that keep to these rules, and one draw needn't show every extreme that they name: `partners`: row s holds 28 different tiles, each within 28 tiles of tile s * 1, counted around the end of the range, except that for even s slot 0 holds tile (s * 1 + 288 // 2) mod 288.
All inputs are finite; a program needn't handle non-finite values.
Results may differ from a plain program's by a relative error of at most 0.00029.
Values sent between devices are 32-bit elements; how exact they have to be, the bound alone decides.
No kernel may reach another device: no remote copies, remote signals or barrier semaphores. Data moves between devices by JAX's collectives and lax.ppermute only.
A program may use at most 128 MiB of HBM per device.

v0:
```python
import functools
import math

import jax
import jax.numpy as jnp
from jax import lax
from jax.experimental import pallas as pl
from jax.experimental.pallas import tpu as pltpu
from jax.sharding import PartitionSpec as P

entropy = 0.1
scale = math.log2(math.e) / entropy
ln2 = math.log(2.0)
nothing = -1e30
floor = -1e25
unit_rows = 64
group = 9
span = 10
ring = 4
f32 = jnp.float32
bf16 = jnp.bfloat16


def pieces(a):
    first = a.astype(bf16).astype(f32)
    rest = a - first
    second = rest.astype(bf16).astype(f32)
    return first, second, rest - second


def extra_rows(bias):
    place = lax.broadcasted_iota(jnp.int32, (64, bias.shape[1]), 0)
    block = jnp.where(place < 3, 1.0, 0.0)
    for k, piece in enumerate(pieces(bias)):
        block = jnp.where(place == 3 + k, piece, block)
    return block.astype(bf16)


def pack_targets(
    count_ref, points_ref, potential_ref, wire_ref, square_ref, line_ref, tally_ref, held_ref, level_ref, sems,
):
    copies = [
        pltpu.make_async_copy(source, target, sems.at[k])
        for k, (source, target) in enumerate(
            ((points_ref, held_ref), (potential_ref, level_ref), (count_ref, tally_ref))
        )
    ]
    for copy in copies:
        copy.start()
    share = held_ref.shape[1]
    tile = 256
    mid = share // 2
    begin = lax.axis_index("row") * share
    first_tile = begin // tile
    offset = begin - first_tile * tile
    last_tile = jnp.minimum(first_tile + 1, tally_ref.shape[0] - 1)
    square_ref[...] = jnp.zeros_like(square_ref)
    line_ref[...] = jnp.full_like(line_ref, nothing)
    wire_ref[mid : mid + 8, :] = jnp.zeros((8, 128), f32)
    for copy in copies:
        copy.wait()
    points = held_ref[...]
    square_ref[0:64, 0:share] = points
    turned = square_ref[...].T
    wire_ref[0:mid, :] = scale * (turned[0:mid] + pltpu.roll(turned[mid:share], 64, 1))
    level = level_ref[...].reshape(1, share)
    level = scale * (level - 0.5 * jnp.sum(points * points, axis=0, keepdims=True))
    spot = offset + lax.broadcasted_iota(jnp.int32, (1, share), 1)
    place = jnp.where(spot < tile, spot, spot - tile)
    bound = jnp.where(spot < tile, tally_ref[first_tile], tally_ref[last_tile])
    line_ref[0:1, 0:share] = jnp.where(place < bound, level, nothing)
    for k in range(3):
        wire_ref[mid + k : mid + k + 1, :] = line_ref[0:1, 128 * k : 128 * (k + 1)]


def unpack_targets(wires, operand_ref):
    lane = lax.broadcasted_iota(jnp.int32, (144, 128), 1)
    front = lane < 64
    sublane = lax.broadcasted_iota(jnp.int32, (16, 384), 0)
    pick_row = lax.broadcasted_iota(jnp.int32, (16, 128), 0)
    pick_lane = lax.broadcasted_iota(jnp.int32, (16, 128), 1)
    pick = jnp.where((pick_lane == pick_row + 64) & (pick_row < 6), 1.0, 0.0).astype(bf16)
    row_here = lax.axis_index("row")
    x_here = row_here // ring
    y_here = row_here - x_here * ring
    even = lax.rem(lax.axis_index("col"), 2) == 0
    for k in range(ring):
        for j in range(ring):
            x = lax.rem(x_here + ring - jnp.where(even, k, j), ring)
            y = lax.rem(y_here + ring - jnp.where(even, j, k), ring)
            a = pl.multiple_of((x * ring + y) * 288, 16)
            b = pl.multiple_of((x * ring + y) * 288 + 144, 16)
            both = wires[k][j, 0:144, :]
            high = both.astype(bf16).astype(f32)
            low = both - high
            high_back = pltpu.roll(high, 64, 1)
            low_back = pltpu.roll(low, 64, 1)
            tail = wires[k][j, 144:152, :]
            line = jnp.concatenate([tail[0:1], tail[1:2], tail[2:3]], axis=1)
            stacked = jnp.where(sublane < 6, 1.0, 0.0)
            for i, piece in enumerate(pieces(line)):
                stacked = jnp.where(sublane == i, piece, stacked)
            extra = lax.dot_general(
                stacked.astype(bf16), pick, (((0,), (0,)), ((), ())), preferred_element_type=f32
            )
            operand_ref[pl.ds(a, 144), 0:128] = jnp.where(front, high, low_back).astype(bf16)
            operand_ref[pl.ds(a, 144), 128:256] = jnp.where(front, high, extra[0:144]).astype(bf16)
            operand_ref[pl.ds(b, 144), 0:128] = jnp.where(front, high_back, low).astype(bf16)
            operand_ref[pl.ds(b, 144), 128:256] = jnp.where(
                front, high_back, extra[144:288]
            ).astype(bf16)
    rows = ring * ring * 288
    dummy_lane = lax.broadcasted_iota(jnp.int32, (unit_rows, 256), 1)
    operand_ref[rows : rows + unit_rows, :] = jnp.where(dummy_lane == 192, nothing, 0.0).astype(bf16)


def load_weights(points_ref, weights_ref, shift):
    tiles, depth, tile = weights_ref.shape
    for s in range(tiles):
        x = points_ref[:, s * tile : (s + 1) * tile]
        high = x.astype(bf16)
        low = (x - high.astype(f32)).astype(bf16)
        bias = (-0.5 * scale) * jnp.sum(x * x, axis=0, keepdims=True)
        moved = 0.0
        if shift is not None:
            moved = jnp.concatenate([shift[2 * s : 2 * s + 1], shift[2 * s + 1 : 2 * s + 2]], axis=1)
        weights_ref[s, 0:64, :] = high
        weights_ref[s, 64:128, :] = high
        weights_ref[s, 128:192, :] = low
        weights_ref[s, 192:256, :] = extra_rows(bias + moved)


def plan_work(count_ref, local_ref, plan_ref):
    src_tiles = local_ref.shape[0] - 6
    per_tile = 256 // unit_rows
    units = count_ref.shape[0] * per_tile
    per = units // group
    unit = lax.broadcasted_iota(jnp.int32, (24, 128), 1)
    tile_of = unit // per_tile
    bound = jnp.zeros((24, 128), jnp.int32)
    for t in range(count_ref.shape[0]):
        bound = jnp.where(tile_of == t, count_ref[t], bound)
    live = bound > (unit - tile_of * per_tile) * unit_rows
    hits = jnp.zeros((24, 128), f32)
    for k in range(local_ref.shape[1]):
        hits = jnp.where(local_ref[:, k : k + 1] == tile_of, 1.0, hits)
    active = jnp.where(live, hits, 0.0)
    down = lax.broadcasted_iota(jnp.int32, (128, 128), 0)
    across = lax.broadcasted_iota(jnp.int32, (128, 128), 1)
    upto = jnp.where(down <= across, 1.0, 0.0).astype(bf16)
    rank = jnp.dot(active.astype(bf16), upto, preferred_element_type=f32)
    counts = jnp.broadcast_to(rank[:, 127:128], (24, 128))
    place = jnp.where(active > 0.0, rank - 1.0, -1.0)
    place = jnp.concatenate([place, jnp.full((104, 128), -1.0, f32)], axis=0).T
    position = across.astype(f32)
    value = (down - units).astype(f32)
    plan_ref[...] = jnp.full_like(plan_ref, units)
    last = lax.broadcasted_iota(jnp.int32, (1, 128), 1)
    chunks = jnp.floor((counts + (group - 0.5)) / group).astype(jnp.int32)
    begin = jnp.zeros((1, 128), jnp.int32)
    items = [jnp.full((1, 128), src_tiles * per, jnp.int32)] * 2
    for s in range(src_tiles):
        listed = jnp.sum(
            jnp.where(place[:, s : s + 1] == position, value, 0.0), axis=0, keepdims=True
        )
        plan_ref[s : s + 1, :] = jnp.where(
            last == 127, counts[s : s + 1], listed + units
        ).astype(jnp.int32)
        for k in range(2):
            along = last + 128 * k - begin
            inside = (along >= 0) & (along < chunks[s : s + 1])
            items[k] = jnp.where(inside, s * per + along, items[k])
        begin = begin + chunks[s : s + 1]
    plan_ref[src_tiles + 1 : src_tiles + 2, :] = items[0]
    plan_ref[src_tiles + 2 : src_tiles + 3, :] = items[1]
    plan_ref[src_tiles + 3 : src_tiles + 4, :] = begin


def pipeline(plan_ref, items, operand_ref, weights_ref, buffers, visit):
    tiles, depth, tile = weights_ref.shape
    per = (operand_ref.shape[0] // unit_rows - 1) // group

    def where(i):
        code = plan_ref[tiles + 1 + i // 128, lax.rem(i, 128)]
        s = code // per
        first = (code - s * per) * group
        return jnp.minimum(s, tiles - 1), [plan_ref[s, first + k] for k in range(group)]

    def step(j, carry):
        for k in range(span):
            s, units = where(span * j + k)
            rows = jnp.concatenate(
                [
                    operand_ref[pl.ds(pl.multiple_of(u * unit_rows, unit_rows), unit_rows), :]
                    for u in units
                ],
                axis=0,
            )
            buffers[k][...] = jnp.dot(rows, weights_ref[s], preferred_element_type=f32)
        for k in range(span):
            visit(*where(span * j + k), buffers[k])
        return carry

    lax.fori_loop(0, (items + span - 1) // span, step, 0)


def on_duty(which):
    row = lax.axis_index("row")
    apart = lax.axis_index("col") - row + 2 - lax.rem(row, 2) + 16
    near = lax.rem(apart, 16) < 4
    return near if which == 0 else jnp.logical_not(near)


def row_pass(
    which, sheet_ref, points_ref, need_ref, w0, w1, w2, w3, lse_ref,
    operand_ref, weights_ref, plan_ref, sem, total_ref, *buffers,
):
    tiles, depth, tile = weights_ref.shape
    lse_ref[...] = jnp.full_like(lse_ref, nothing)
    copy = pltpu.make_async_copy(sheet_ref, plan_ref, sem)

    def put(s, line):
        lse_ref[pl.ds(2 * s, 1), :] = line[:, 0:128]
        lse_ref[pl.ds(2 * s + 1, 1), :] = line[:, 128:256]

    def work():
        items = plan_ref[tiles + 3, 0]
        unpack_targets((w0, w1, w2, w3), operand_ref)
        total_ref[...] = jnp.zeros_like(total_ref)

        def visit(s, units, buffer):
            part = jnp.exp2(buffer[...]).reshape(4, unit_rows * group // 32, 8, tile)
            total_ref[s] += jnp.sum(jnp.sum(part, axis=1), axis=0)

        pipeline(plan_ref, items, operand_ref, weights_ref, buffers, visit)
        total = jnp.sum(total_ref[...], axis=1)
        lines = jnp.where(total > 0.0, jnp.log2(jnp.maximum(total, 1e-37)), nothing)
        for s in range(tiles):
            put(s, lines[s : s + 1, :])
        fine = (total > 1e-25) & (total < 1e30)
        bad = jnp.where(fine, 0.0, need_ref[...])

        @pl.when(jnp.max(bad) > 0.0)
        def _():
            def one_tile(s, carry):
                weights = weights_ref[s]

                def step(i, state):
                    high, total = state
                    unit = plan_ref[s, i]
                    rows = operand_ref[
                        pl.ds(pl.multiple_of(unit * unit_rows, unit_rows), unit_rows), :
                    ]
                    score = jnp.dot(rows, weights, preferred_element_type=f32)
                    score = score.reshape(unit_rows // 8, 8, tile)
                    new = jnp.maximum(high, jnp.max(score, axis=0))
                    total = total * jnp.exp2(high - new)
                    return new, total + jnp.sum(jnp.exp2(score - new[None]), axis=0)

                start = (jnp.full((8, tile), floor, f32), jnp.zeros((8, tile), f32))
                high, total = lax.fori_loop(0, plan_ref[s, 127], step, start)
                top = jnp.max(high, axis=0, keepdims=True)
                total = jnp.sum(total * jnp.exp2(high - top), axis=0, keepdims=True)
                put(s, jnp.where(total > 0.0, top + jnp.log2(jnp.maximum(total, 1e-37)), nothing))
                return carry

            lax.fori_loop(0, tiles, one_tile, 0)

    @pl.when(on_duty(which))
    def _():
        copy.start()
        load_weights(points_ref, weights_ref, None)
        copy.wait()
        pl.when(plan_ref[tiles + 3, 0] > 0)(work)


def column_pass(
    which, sheet_ref, points_ref, need_ref, w0, w1, w2, w3, lse_ref, mass_ref, other_ref, out_ref,
    operand_ref, weights_ref, plan_ref, sem, total_ref, high_ref, *buffers,
):
    tiles, depth, tile = weights_ref.shape
    out_ref[...] = other_ref[...]
    copy = pltpu.make_async_copy(sheet_ref, plan_ref, sem)

    def work():
        items = plan_ref[tiles + 3, 0]
        unpack_targets((w0, w1, w2, w3), operand_ref)
        total_ref[...] = jnp.zeros_like(total_ref)

        def visit(s, units, buffer):
            for k, u in enumerate(units):
                where = pl.ds(pl.multiple_of(u * unit_rows, unit_rows), unit_rows)
                part = jnp.exp2(buffer[k * unit_rows : (k + 1) * unit_rows, :])
                total_ref[where, :] += part[:, 0:128] + part[:, 128:256]

        pipeline(plan_ref, items, operand_ref, weights_ref, buffers, visit)
        eye = lax.broadcasted_iota(jnp.int32, (128, 128), 0) == lax.broadcasted_iota(
            jnp.int32, (128, 128), 1
        )

        def to_row(column):
            return jnp.sum(jnp.where(eye, column, 0.0), axis=0, keepdims=True)

        bad = jnp.zeros((1, 128), f32)
        for u in range(out_ref.shape[0]):
            sums = to_row(jnp.sum(total_ref[u * 128 : (u + 1) * 128, :], axis=1, keepdims=True))
            out_ref[u : u + 1, :] = jnp.where(
                sums > 0.0, jnp.log2(jnp.maximum(sums, 1e-37)), nothing
            )
            bad = jnp.maximum(bad, jnp.where(sums > 1e-25, 0.0, need_ref[u : u + 1, :]))

        @pl.when(jnp.max(bad) > 0.0)
        def _():
            total_ref[...] = jnp.zeros_like(total_ref)
            high_ref[...] = jnp.full_like(high_ref, floor)

            def one_tile(s, carry):
                def step(i, inner):
                    unit = plan_ref[s, i]
                    where = pl.ds(pl.multiple_of(unit * unit_rows, unit_rows), unit_rows)
                    score = jnp.dot(
                        operand_ref[where, :], weights_ref[s], preferred_element_type=f32
                    )
                    a, b = score[:, 0:128], score[:, 128:256]
                    old = high_ref[where, :]
                    new = jnp.maximum(old, jnp.maximum(a, b))
                    high_ref[where, :] = new
                    total_ref[where, :] = (
                        total_ref[where, :] * jnp.exp2(old - new)
                        + jnp.exp2(a - new)
                        + jnp.exp2(b - new)
                    )
                    return inner

                lax.fori_loop(0, plan_ref[s, 127], step, 0)
                return carry

            lax.fori_loop(0, tiles, one_tile, 0)

            def finish(u, carry):
                where = pl.ds(pl.multiple_of(u * 128, 128), 128)
                high = high_ref[where, :]
                top = jnp.max(high, axis=1, keepdims=True)
                rest = total_ref[where, :] * jnp.exp2(high - top)
                sums = to_row(jnp.sum(rest, axis=1, keepdims=True))
                out_ref[pl.ds(u, 1), :] = jnp.where(
                    sums > 0.0, to_row(top) + jnp.log2(jnp.maximum(sums, 1e-37)), nothing
                )
                return carry

            lax.fori_loop(0, out_ref.shape[0], finish, 0)

    @pl.when(on_duty(which))
    def _():
        copy.start()
        load_weights(points_ref, weights_ref, mass_ref[...] - lse_ref[...])
        copy.wait()
        pl.when(plan_ref[tiles + 3, 0] > 0)(work)


def log_sum(parts):
    top = functools.reduce(jnp.maximum, parts)
    total = sum(jnp.exp2(p - top) for p in parts)
    return top + jnp.log2(total)


def roles(parity, cols):
    four = [d % cols for d in ((-2, -1, 0, 1), (-1, 0, 1, 2))[parity]]
    lead = [0, (1, -1)[parity] % cols]
    near = lead + [d for d in four if d not in lead]
    out = [(2, -2)[parity] % cols, cols // 2]
    begin = four[0]
    out += [(begin + 5) % cols, (begin + 6) % cols]
    return near, out + [d for d in range(cols) if d not in near and d not in out]


def filled(hops, count, cols):
    found = dict(hops)
    back = {d: s for s, d in hops}
    for rank in range(4):
        free = [d for d in range(count) if d not in back]
        for s in [s for s in range(count) if s not in found]:
            if rank == 0:
                picks = [back[s]] if s in back and back[s] in free else []
            elif rank == 1:
                picks = [s ^ 1] if s ^ 1 in free else []
            else:
                picks = [d for d in free if d != s and (d // cols == s // cols or rank == 3)]
                picks.sort(key=lambda d: min((d - s) % cols, (s - d) % cols))
            if picks:
                found[s] = picks[0]
                back[picks[0]] = s
                free.remove(picks[0])
    return sorted(found.items())


def shards(src_points, dst_points, dst_potential, partners, partner_count, src_count, dst_count):
    src_tiles = src_count.shape[0]
    dst_tiles = dst_count.shape[0]
    tile = src_points.shape[0] // src_tiles
    slots = partners.shape[1]
    rows = lax.axis_size("row")
    cols = lax.axis_size("col")
    row_here = lax.axis_index("row")
    col_here = lax.axis_index("col")
    share = dst_points.shape[0]
    points = dst_tiles * tile
    smem = pl.BlockSpec(memory_space=pltpu.SMEM)
    vmem = pl.BlockSpec(memory_space=pltpu.VMEM)
    anywhere = pl.BlockSpec(memory_space=pl.ANY)
    params = pltpu.CompilerParams(vmem_limit_bytes=24 * 1024 * 1024)
    places = [roles(r % 2, cols) for r in range(rows)]
    near = [[(r + d) % cols for d in places[r][0]] for r in range(rows)]
    far = [[(r + d) % cols for d in places[r][1]] for r in range(rows)]
    parity = lax.rem(row_here, 2)
    apart = lax.rem(col_here - row_here + 2 - parity + cols, cols)
    in_near = apart < 4
    in_far = (
        (apart == 5)
        | (apart == 6)
        | (apart == jnp.where(parity == 0, 4, cols - 1))
        | (apart == jnp.where(parity == 0, 10, 9))
    )

    def send(a, hops, full=True):
        hops = [(s[0] * cols + s[1], d[0] * cols + d[1]) for s, d in hops]
        return lax.ppermute(a, ("row", "col"), filled(hops, rows * cols, cols) if full else hops)

    every = [(r, c) for r in range(rows) for c in range(cols)]

    wire = pl.pallas_call(
        pack_targets,
        out_shape=jax.ShapeDtypeStruct((share // 2 + 8, 128), f32),
        in_specs=[anywhere] * 3,
        out_specs=vmem,
        scratch_shapes=[
            pltpu.VMEM((128, 384), f32),
            pltpu.VMEM((8, 384), f32),
            pltpu.SMEM((dst_tiles,), jnp.int32),
            pltpu.VMEM((64, share), f32),
            pltpu.VMEM((share,), f32),
            pltpu.SemaphoreType.DMA((3,)),
        ],
        compiler_params=pltpu.CompilerParams(vmem_limit_bytes=60 * 1024 * 1024),
    )(dst_count, dst_points.T, dst_potential)

    def around(r, dx, dy):
        return (r // ring + dx) % ring * ring + (r + dy) % ring

    def first_hop(r, c, k):
        return around(r, 0, k) if c % 2 == 0 else around(r, k, 0)

    def second_hop(r, c, k):
        return around(r, k, 0) if c % 2 == 0 else around(r, 0, k)

    bundle = jnp.stack(
        [wire]
        + [send(wire, [((r, c), (first_hop(r, c, k), c)) for r, c in every]) for k in (1, 2, 3)]
    )
    busy = [set(near[r] + far[r][:2]) for r in range(rows)]
    slot_on = jnp.arange(slots, dtype=jnp.int32)[None, :] < partner_count[:, None]
    local = jnp.where(slot_on, partners - col_here * dst_tiles, -1)
    plan = pl.pallas_call(
        plan_work,
        out_shape=jax.ShapeDtypeStruct((24, 128), jnp.int32),
        in_specs=[smem, vmem],
        out_specs=vmem,
        compiler_params=params,
    )(dst_count, jnp.pad(local, ((0, 24 - src_tiles), (0, 0)), constant_values=-1))
    plan, local, dst_count, src_count, bundle = lax.optimization_barrier(
        (plan, local, dst_count, src_count, bundle)
    )
    wires = [bundle] + [
        send(
            bundle,
            [
                ((r, c), (second_hop(r, c, k), c))
                for r, c in every
                if c in busy[second_hop(r, c, k)]
            ],
            full=False,
        )
        for k in (1, 2, 3)
    ]
    place = jnp.arange(tile, dtype=jnp.int32)
    src_live = place[None, :] < src_count[:, None]
    dst_live = place[None, :] < dst_count[:, None]
    wanted = jnp.any(local[:, :, None] == jnp.arange(dst_tiles, dtype=jnp.int32), axis=1)
    src_need = jnp.where(src_live & jnp.any(wanted, axis=1)[:, None], 1.0, 0.0)
    dst_need = jnp.where(dst_live & jnp.any(wanted, axis=0)[:, None], 1.0, 0.0)
    dst_need = dst_need.reshape(points // 128, 128)
    counted = jnp.repeat(src_count.astype(f32), 2)
    half_live = (place[:128][None, :] + 128 * (jnp.arange(2 * src_tiles) % 2)[:, None]) < jnp.repeat(
        src_count, 2
    )[:, None]
    all_src = src_tiles * rows
    mass = jnp.where(half_live, -jnp.log2(counted)[:, None] - math.log2(all_src), nothing)

    scratch = [
        pltpu.VMEM((points + unit_rows, 256), bf16),
        pltpu.VMEM((src_tiles, 256, tile), bf16),
    ]
    buffers = [pltpu.VMEM((unit_rows * group, tile), f32)] * span
    heavy = pl.CostEstimate(flops=8_000_000_000, bytes_accessed=4_000_000, transcendentals=8_000_000)
    light = pl.CostEstimate(flops=100_000_000, bytes_accessed=100_000, transcendentals=100_000)
    turned = src_points.T

    halves = 2 * src_tiles
    scratch += [pltpu.SMEM((24, 128), jnp.int32), pltpu.SemaphoreType.DMA]

    def sum_rows(which, cost):
        return pl.pallas_call(
            functools.partial(row_pass, which),
            out_shape=jax.ShapeDtypeStruct((halves, tile // 2), f32),
            in_specs=[anywhere] + [vmem] * (2 + ring),
            out_specs=vmem,
            scratch_shapes=scratch + [pltpu.VMEM((src_tiles, 8, tile), f32)] + buffers,
            compiler_params=params,
            cost_estimate=cost,
        )(plan, turned, src_need, *wires)

    def sum_columns(which, lse, other, cost):
        return pl.pallas_call(
            functools.partial(column_pass, which),
            out_shape=jax.ShapeDtypeStruct((points // 128, 128), f32),
            in_specs=[anywhere] + [vmem] * (5 + ring),
            out_specs=vmem,
            scratch_shapes=scratch + [pltpu.VMEM((points + unit_rows, 128), f32)] * 2 + buffers,
            compiler_params=params,
            cost_estimate=cost,
        )(plan, turned, dst_need, *wires, lse, mass, other)

    far_lse = sum_rows(1, light)
    early = send(
        far_lse,
        [((r, far[r][k]), (r, near[r][k])) for r in range(rows) for k in (0, 1)],
        full=False,
    )
    near_lse = sum_rows(0, heavy)
    got_early = (col_here == row_here) | (col_here == row_here + 1 - 2 * parity)
    lse = log_sum([near_lse, jnp.where(got_early, early, nothing)])

    def pairs(test):
        return [((r, c), (r, d)) for r in range(rows) for c in near[r] for d in near[r] if test(c, d)]

    lse = log_sum(
        [
            lse,
            send(lse, [((r, c), (r, c ^ 1)) for r, c in every]),
            send(lse, pairs(lambda c, d: (c - d) % cols in (2, cols - 2))),
            send(lse, pairs(lambda c, d: (c - (d ^ 1)) % cols in (2, cols - 2))),
        ]
    )
    spread = send(lse, [((r, near[r][k]), (r, far[r][k])) for r in range(rows) for k in range(4)])
    blank = jnp.full((points // 128, 128), nothing, f32)
    near_part = sum_columns(0, lse, blank, heavy)
    col_part = sum_columns(1, spread, near_part, light)
    known = jnp.where(in_far, spread, lse)
    known, near_part = lax.optimization_barrier((known, near_part))
    rest = send(
        known,
        [((r, (near[r] + far[r])[k]), (r, far[r][4 + k])) for r in range(rows) for k in range(8)],
    )
    shared_out = lax.all_to_all(col_part.reshape(rows, share), "row", 0, 0)

    row_lse = jnp.where(in_near | in_far, known, rest)
    src_potential = jnp.where(
        half_live,
        entropy * (-jnp.log(counted)[:, None] - math.log(all_src) - ln2 * row_lse),
        0.0,
    ).reshape(-1)

    spot = row_here * share + jnp.arange(share, dtype=jnp.int32)
    spot_tile = spot // tile
    spot_count = jnp.sum(
        jnp.where(
            spot_tile[:, None] == jnp.arange(dst_tiles, dtype=jnp.int32)[None, :],
            dst_count[None, :],
            0,
        ),
        axis=1,
    )
    top = jnp.max(shared_out, axis=0)
    col_log = top + jnp.log2(jnp.sum(jnp.exp2(shared_out - top[None]), axis=0))
    dst_new = jnp.where(
        (spot - spot_tile * tile < spot_count) & (top > 0.5 * nothing),
        entropy
        * (-jnp.log(spot_count.astype(f32)) - math.log(dst_tiles * cols) - ln2 * col_log)
        + dst_potential,
        0.0,
    )
    return src_potential, dst_new


def solution(mesh):
    in_specs = (
        P("row", None),
        P(("col", "row"), None),
        P(("col", "row")),
        P("row", None),
        P("row"),
        P("row"),
        P("col"),
    )
    out_specs = (P("row"), P(("col", "row")))
    return jax.shard_map(shards, mesh=mesh, in_specs=in_specs, out_specs=out_specs, check_vma=False)
```

profile of v0, /device:TPU:6, one launch (start us, length us, event | category | flops | bytes accessed | tf_op | source)
XLA Modules:
  0.0 209.8 jit_solution(16753182073314731741)
XLA Ops:
  0.6 0.0 copy-start
  0.6 1.8 shard_map.87
  2.5 1.7 collective-permute-start
  4.1 2.9 %collective-permute-start.1 = (f32[152,128]{1,0:T(8,128)}, f32[152,128]{1,0:T(8,128)S(1)}, u32[]{:S(2)}, u32[]{:S(2)}) collective-permute-start(f32[152,128]{1,0:T(8,128)} %shard_map.87), channel_id=1, source_target_pairs={{0,32},{1,129},{2,34},{3,131},{4,36},{5,133},{6,38},{7,135},{8,40}... | collective-permute-start | bytes 233480 | tf_op jit(solution)/shard_map/ppermute | solution.py:427
  7.0 1.3 collective-permute-start.2
  8.4 0.8 subtract_select_fusion
  9.2 0.0 copy-start.1
  9.2 0.6 copy-done.1
  9.8 1.4 shard_map.86.sheet_ref
  11.3 0.0 collective-permute-done
  11.4 0.0 collective-permute-done.1
  11.4 0.3 collective-permute-done.2
  11.6 0.9 pad_maximum_fusion.w0
  12.6 2.6 %collective-permute-start.3 = (f32[4,152,128]{2,1,0:T(8,128)S(1)}, f32[4,152,128]{2,1,0:T(8,128)S(1)}, u32[]{:S(2)}, u32[]{:S(2)}) collective-permute-start(f32[4,152,128]{2,1,0:T(8,128)S(1)} %pad_maximum_fusion.w0), channel_id=1, source_target_pairs={{1,17},{2,66},{3,19},{4,68},{6,70},{9,25},{12,76},{15,31},{17,33},... | collective-permute-start | bytes 933896 | tf_op jit(solution)/shard_map/ppermute | solution.py:427
  15.1 0.7 collective-permute-start.4
  15.8 3.4 %collective-permute-start.5 = (f32[4,152,128]{2,1,0:T(8,128)S(1)}, f32[4,152,128]{2,1,0:T(8,128)S(1)}, u32[]{:S(2)}, u32[]{:S(2)}) collective-permute-start(f32[4,152,128]{2,1,0:T(8,128)S(1)} %pad_maximum_fusion.w0), channel_id=1, source_target_pairs={{1,49},{3,51},{4,196},{5,53},{10,202},{11,59},{12,204},{14,206},{1... | collective-permute-start | bytes 933896 | tf_op jit(solution)/shard_map/ppermute | solution.py:427
  19.2 0.5 fusion
  19.7 0.7 fusion.6.need_ref
  20.4 0.7 negate_add_fusion.1
  21.1 0.1 broadcast_in_dim.85
  21.1 0.1 sub.92
  21.2 0.7 broadcast_in_dim.78
  22.0 0.1 lt.78
  22.0 0.7 lt.90
  22.8 0.1 lt.91
  22.9 0.1 and.56
  22.9 0.1 and.57
  23.0 0.1 fusion.9
  23.1 0.0 collective-permute-done.3.w1
  23.2 0.0 collective-permute-done.4.w2
  23.2 0.4 collective-permute-done.5.w3
  23.6 0.0 copy-done
  23.6 0.8 shard_map.89
  24.3 0.0 copy-start.2
  24.4 0.7 collective-permute-start.6
  25.1 0.0 collective-permute-done.6
  25.1 0.2 collective-permute-start.7
  25.3 0.4 collective-permute-start.8
  25.7 0.1 collective-permute-start.9
  25.9 0.0 copy-done.2
  25.9 0.1 select_reduce_fusion
  25.9 0.1 broadcast_in_dim.79
  26.0 0.1 sub.80
  26.1 0.3 collective-permute-done.7
  26.4 0.2 collective-permute-done.8
  26.6 0.3 collective-permute-done.9
  26.9 82.8 %collective-permute-start.10 = (f32[36,128]{1,0:T(8,128)S(1)}, f32[36,128]{1,0:T(8,128)S(1)}, u32[]{:S(2)}, u32[]{:S(2)}) collective-permute-start(f32[36,128]{1,0:T(8,128)S(1)} %multiply_add_fusion.lse_ref), channel_id=1, source_target_pairs={{0,2},{1,8},{2,0},{3,14},{4,15},{5,9},{6,7},{7,6},{8,1},{9,5},{10,... | collective-permute-start | bytes 55304 | tf_op jit(solution)/shard_map/ppermute | solution.py:427
  109.8 0.0 copy-start.3
  109.8 1.4 collective-permute-done.10.lse_ref
  111.2 0.8 shard_map.91
  112.0 0.7 all_to_all.11
  112.7 84.4 %all-to-all-start = ((f32[16,1,288]{2,1,0:T(1,128)}), f32[16,1,288]{2,1,0:T(1,128)S(1)}, u32[]{:S(2)}, u32[]{:S(2)}) async-start(f32[16,1,288]{2,1,0:T(1,128)} %all_to_all.11), calls=%async_computation | async-start | bytes 49152 | tf_op jit(solution)/shard_map/all_to_all | solution.py:564
  197.1 10.5 %collective-permute-start.11 = (f32[36,128]{1,0:T(8,128)S(1)}, f32[36,128]{1,0:T(8,128)S(1)}, u32[]{:S(2)}, u32[]{:S(2)}) collective-permute-start(f32[36,128]{1,0:T(8,128)S(1)} %broadcast_select_fusion), channel_id=1, source_target_pairs={{0,5},{1,6},{2,10},{3,12},{4,13},{5,0},{6,1},{7,14},{8,11},{9,15},... | collective-permute-start | bytes 55304 | tf_op jit(solution)/shard_map/ppermute | solution.py:427
  207.6 0.0 all-to-all-done
  207.6 0.0 copy-done.3
  207.7 0.6 add_select_fusion.1
  208.3 0.8 collective-permute-done.11
  209.1 0.7 select_bitcast_fusion
  (16 shorter events, 0.3 us)
Async XLA Ops:
  0.6 23.0 %copy-start = (f32[4608,64]{0,1:T(8,128)S(1)}, f32[4608,64]{0,1:T(8,128)}, u32[]{:S(2)}) copy-start(f32[4608,64]{0,1:T(8,128)} %param.7) | copy-start | bytes 3538948
  2.5 8.9 %collective-permute-start = (f32[152,128]{1,0:T(8,128)}, f32[152,128]{1,0:T(8,128)S(1)}, u32[]{:S(2)}, u32[]{:S(2)}) collective-permute-start(f32[152,128]{1,0:T(8,128)} %shard_map.87), channel_id=1, source_target_pairs={{0,16},{1,65},{2,18},{3,67},{4,20},{5,69},{6,22},{7,71},{8,24},{9,... | collective-permute-start | bytes 233480 | tf_op jit(solution)/shard_map/ppermute | solution.py:427
  4.1 7.2 %collective-permute-start.1 = (f32[152,128]{1,0:T(8,128)}, f32[152,128]{1,0:T(8,128)S(1)}, u32[]{:S(2)}, u32[]{:S(2)}) collective-permute-start(f32[152,128]{1,0:T(8,128)} %shard_map.87), channel_id=1, source_target_pairs={{0,32},{1,129},{2,34},{3,131},{4,36},{5,133},{6,38},{7,135},{8,40}... | collective-permute-start | bytes 233480 | tf_op jit(solution)/shard_map/ppermute | solution.py:427
  7.0 4.6 %collective-permute-start.2 = (f32[152,128]{1,0:T(8,128)}, f32[152,128]{1,0:T(8,128)S(1)}, u32[]{:S(2)}, u32[]{:S(2)}) collective-permute-start(f32[152,128]{1,0:T(8,128)} %shard_map.87), channel_id=1, source_target_pairs={{0,48},{1,193},{2,50},{3,195},{4,52},{5,197},{6,54},{7,199},{8,56}... | collective-permute-start | bytes 233480 | tf_op jit(solution)/shard_map/ppermute | solution.py:427
  9.2 0.7 copy-start.1
  12.6 10.6 %collective-permute-start.3 = (f32[4,152,128]{2,1,0:T(8,128)S(1)}, f32[4,152,128]{2,1,0:T(8,128)S(1)}, u32[]{:S(2)}, u32[]{:S(2)}) collective-permute-start(f32[4,152,128]{2,1,0:T(8,128)S(1)} %pad_maximum_fusion.w0), channel_id=1, source_target_pairs={{1,17},{2,66},{3,19},{4,68},{6,70},{9,25},{12,76},{15,31},{17,33},... | collective-permute-start | bytes 933896 | tf_op jit(solution)/shard_map/ppermute | solution.py:427
  15.1 8.0 %collective-permute-start.4 = (f32[4,152,128]{2,1,0:T(8,128)S(1)}, f32[4,152,128]{2,1,0:T(8,128)S(1)}, u32[]{:S(2)}, u32[]{:S(2)}) collective-permute-start(f32[4,152,128]{2,1,0:T(8,128)S(1)} %pad_maximum_fusion.w0), channel_id=1, source_target_pairs={{0,128},{1,33},{3,35},{6,134},{8,136},{10,138},{17,49},{19,51},{21... | collective-permute-start | bytes 933896 | tf_op jit(solution)/shard_map/ppermute | solution.py:427
  15.8 7.8 %collective-permute-start.5 = (f32[4,152,128]{2,1,0:T(8,128)S(1)}, f32[4,152,128]{2,1,0:T(8,128)S(1)}, u32[]{:S(2)}, u32[]{:S(2)}) collective-permute-start(f32[4,152,128]{2,1,0:T(8,128)S(1)} %pad_maximum_fusion.w0), channel_id=1, source_target_pairs={{1,49},{3,51},{4,196},{5,53},{10,202},{11,59},{12,204},{14,206},{1... | collective-permute-start | bytes 933896 | tf_op jit(solution)/shard_map/ppermute | solution.py:427
  24.3 1.5 copy-start.2
  24.4 0.7 collective-permute-start.6
  25.1 1.3 collective-permute-start.7
  25.3 1.2 collective-permute-start.8
  25.7 1.2 collective-permute-start.9
  26.9 84.3 %collective-permute-start.10 = (f32[36,128]{1,0:T(8,128)S(1)}, f32[36,128]{1,0:T(8,128)S(1)}, u32[]{:S(2)}, u32[]{:S(2)}) collective-permute-start(f32[36,128]{1,0:T(8,128)S(1)} %multiply_add_fusion.lse_ref), channel_id=1, source_target_pairs={{0,2},{1,8},{2,0},{3,14},{4,15},{5,9},{6,7},{7,6},{8,1},{9,5},{10,... | collective-permute-start | bytes 55304 | tf_op jit(solution)/shard_map/ppermute | solution.py:427
  109.8 97.9 %copy-start.3 = (f32[288]{0:T(512)S(1)}, f32[288]{0:T(512)}, u32[]{:S(2)}) copy-start(f32[288]{0:T(512)} %potential_ref.1) | copy-start | bytes 3460
  112.7 94.9 %all-to-all-start = ((f32[16,1,288]{2,1,0:T(1,128)}), f32[16,1,288]{2,1,0:T(1,128)S(1)}, u32[]{:S(2)}, u32[]{:S(2)}) async-start(f32[16,1,288]{2,1,0:T(1,128)} %all_to_all.11), calls=%async_computation | async-start | bytes 49152 | tf_op jit(solution)/shard_map/all_to_all | solution.py:564
  197.1 12.0 %collective-permute-start.11 = (f32[36,128]{1,0:T(8,128)S(1)}, f32[36,128]{1,0:T(8,128)S(1)}, u32[]{:S(2)}, u32[]{:S(2)}) collective-permute-start(f32[36,128]{1,0:T(8,128)S(1)} %broadcast_select_fusion), channel_id=1, source_target_pairs={{0,5},{1,6},{2,10},{3,12},{4,13},{5,0},{6,1},{7,14},{8,11},{9,15},... | collective-permute-start | bytes 55304 | tf_op jit(solution)/shard_map/ppermute | solution.py:427
where the time goes:
time: 211 us; the launch traced here: 210 us
  starting transfers between devices  192 us (91%)
  other arithmetic  5.18 us (2%)
  Pallas kernels  4.76 us (2%)
  waiting for transfers between devices  3.76 us (2%)
  local copies, waits for them, and re-layouts  3.55 us (2%)
    ppermute x12, starting transfers between devices, send(): lax.ppermute(a, ('row', 'col'), filled(hops, rows * cols, cols) if full e...  107 us
    all_to_all x1, starting transfers between devices, shards(): shared_out = lax.all_to_all(col_part.reshape(rows, share), 'row', 0, 0)  84.4 us
  transfers between devices with their start and end apart: 13, of which 7 were waited for; matrix products, arithmetic and copies ran while one was open for 3% of the time, Pallas kernels for 1%

commit v1 on v0

--- a/solution.py
+++ b/solution.py
@@ -71,6 +71,11 @@
     line_ref[0:1, 0:share] = jnp.where(place < bound, level, nothing)
     for k in range(3):
         wire_ref[mid + k : mid + k + 1, :] = line_ref[0:1, 128 * k : 128 * (k + 1)]
+
+
+def join(a_ref, b_ref, c_ref, d_ref, out_ref):
+    for k, ref in enumerate((a_ref, b_ref, c_ref, d_ref)):
+        out_ref[k] = ref[...]
 
 
 def unpack_targets(wires, operand_ref):
@@ -453,10 +458,13 @@
     def second_hop(r, c, k):
         return around(r, k, 0) if c % 2 == 0 else around(r, 0, k)
 
-    bundle = jnp.stack(
-        [wire]
-        + [send(wire, [((r, c), (first_hop(r, c, k), c)) for r, c in every]) for k in (1, 2, 3)]
-    )
+    bundle = pl.pallas_call(
+        join,
+        out_shape=jax.ShapeDtypeStruct((ring,) + wire.shape, f32),
+        in_specs=[vmem] * ring,
+        out_specs=vmem,
+        compiler_params=params,
+    )(wire, *[send(wire, [((r, c), (first_hop(r, c, k), c)) for r, c in every]) for k in (1, 2, 3)])
     busy = [set(near[r] + far[r][:2]) for r in range(rows)]
     slot_on = jnp.arange(slots, dtype=jnp.int32)[None, :] < partner_count[:, None]
     local = jnp.where(slot_on, partners - col_here * dst_tiles, -1)
@@ -531,11 +539,10 @@
         )(plan, turned, dst_need, *wires, lse, mass, other)
 
     far_lse = sum_rows(1, light)
-    early = send(
-        far_lse,
-        [((r, far[r][k]), (r, near[r][k])) for r in range(rows) for k in (0, 1)],
-        full=False,
-    )
+    loops = [
+        [(r, c) for c in (far[r][k], near[r][k], far[r][k] ^ 1)] for r in range(rows) for k in (0, 1)
+    ]
+    early = send(far_lse, [(loop[i], loop[(i + 1) % 3]) for loop in loops for i in range(3)])
     near_lse = sum_rows(0, heavy)
     got_early = (col_here == row_here) | (col_here == row_here + 1 - 2 * parity)
     lse = log_sum([near_lse, jnp.where(got_early, early, nothing)])

time: 211 us -> 211 us (level)
  the two profiles are of different devices: /device:TPU:6 before, /device:TPU:20 now
where the time goes in v1:
time: 211 us
  starting transfers between devices  190 us (90%)
  waiting for transfers between devices  7.03 us (3%)
  Pallas kernels  4.77 us (2%)
  local copies, waits for them, and re-layouts  4.43 us (2%)
  other arithmetic  4.26 us (2%)
    all_to_all x1, starting transfers between devices, shards(): shared_out = lax.all_to_all(col_part.reshape(rows, share), 'row', 0, 0)  146 us
    ppermute x12, starting transfers between devices, send(): lax.ppermute(a, ('row', 'col'), filled(hops, rows * cols, cols) if full e...  43.2 us
    ppermute x12, waiting for transfers between devices, send(): lax.ppermute(a, ('row', 'col'), filled(hops, rows * cols, cols) if full e...  7.03 us
  transfers between devices with their start and end apart: 13, of which 9 were waited for; matrix products, arithmetic and copies ran while one was open for 3% of the time, Pallas kernels for 1%

profile of v1, /device:TPU:20, one launch (start us, length us, event | category | flops | bytes accessed | tf_op | source)
XLA Modules:
  0.0 211.0 jit_solution(5226745241625104384)
XLA Ops:
  0.6 0.0 copy-start
  0.6 1.8 shard_map.87.a_ref
  2.5 1.4 collective-permute-start
  3.8 0.6 collective-permute-start.1
  4.5 1.1 collective-permute-start.2
  5.5 0.8 subtract_select_fusion
  6.3 0.0 copy-start.2
  6.3 0.6 copy-done.2
  7.0 1.4 shard_map.86.sheet_ref
  8.5 0.0 collective-permute-done.b_ref
  8.5 1.5 collective-permute-done.1.c_ref
  9.9 0.1 collective-permute-done.2.d_ref
  10.1 0.0 copy-start.1
  10.1 0.9 copy-done.1
  11.0 3.1 %collective-permute-start.3 = (f32[4,152,128]{2,1,0:T(8,128)S(1)}, f32[4,152,128]{2,1,0:T(8,128)S(1)}, u32[]{:S(2)}, u32[]{:S(2)}) collective-permute-start(f32[4,152,128]{2,1,0:T(8,128)S(1)} %shard_map.88.w0), channel_id=1, source_target_pairs={{1,17},{2,66},{3,19},{4,68},{6,70},{9,25},{12,76},{15,31},{17,33},... | collective-permute-start | bytes 933896 | tf_op jit(solution)/shard_map/ppermute | solution.py:432
  14.1 1.3 collective-permute-start.4
  15.4 0.7 collective-permute-start.5
  16.1 0.5 fusion
  16.6 0.7 fusion.6.need_ref
  17.3 0.7 negate_add_fusion.1
  18.0 0.1 broadcast_in_dim.85
  18.0 0.1 sub.92
  18.1 0.7 broadcast_in_dim.78
  18.9 0.1 lt.78
  18.9 0.7 lt.90
  19.7 0.1 lt.91
  19.8 0.1 and.56
  19.8 0.1 and.57
  19.9 0.1 fusion.9
  20.1 0.0 collective-permute-done.3.w1
  20.1 1.8 collective-permute-done.4.w2
  21.8 0.0 collective-permute-done.5.w3
  21.8 0.0 copy-done
  21.8 0.8 shard_map.90
  22.6 0.0 copy-start.3
  22.6 0.1 collective-permute-start.6
  22.7 1.1 collective-permute-done.6
  23.9 0.3 collective-permute-start.7
  24.1 0.3 collective-permute-start.8
  24.5 0.2 collective-permute-start.9
  24.7 0.0 copy-done.3
  24.7 0.1 select_reduce_fusion
  24.7 0.1 broadcast_in_dim.79
  24.8 0.1 sub.80
  24.9 0.3 collective-permute-done.7
  25.2 0.2 collective-permute-done.8
  25.3 0.3 collective-permute-done.9
  25.7 0.4 collective-permute-start.10
  26.2 0.0 copy-start.4
  26.2 1.0 collective-permute-done.10.lse_ref
  27.2 0.8 shard_map.92
  27.9 0.7 all_to_all.11
  28.6 146.4 %all-to-all-start = ((f32[16,1,288]{2,1,0:T(1,128)}), f32[16,1,288]{2,1,0:T(1,128)S(1)}, u32[]{:S(2)}, u32[]{:S(2)}) async-start(f32[16,1,288]{2,1,0:T(1,128)} %all_to_all.11), calls=%async_computation | async-start | bytes 49152 | tf_op jit(solution)/shard_map/all_to_all | solution.py:571
  175.0 33.8 %collective-permute-start.11 = (f32[36,128]{1,0:T(8,128)S(1)}, f32[36,128]{1,0:T(8,128)S(1)}, u32[]{:S(2)}, u32[]{:S(2)}) collective-permute-start(f32[36,128]{1,0:T(8,128)S(1)} %broadcast_select_fusion), channel_id=1, source_target_pairs={{0,5},{1,6},{2,10},{3,12},{4,13},{5,0},{6,1},{7,14},{8,11},{9,15},... | collective-permute-start | bytes 55304 | tf_op jit(solution)/shard_map/ppermute | solution.py:432
  208.8 0.0 all-to-all-done
  208.9 0.0 copy-done.4
  208.9 0.6 add_select_fusion.1
  209.5 0.8 collective-permute-done.11
  210.3 0.7 select_bitcast_fusion
  (17 shorter events, 0.3 us)
Async XLA Ops:
  0.6 21.2 %copy-start = (f32[4608,64]{0,1:T(8,128)S(1)}, f32[4608,64]{0,1:T(8,128)}, u32[]{:S(2)}) copy-start(f32[4608,64]{0,1:T(8,128)} %param.7) | copy-start | bytes 3538948
  2.5 6.0 %collective-permute-start = (f32[152,128]{1,0:T(8,128)}, f32[152,128]{1,0:T(8,128)S(1)}, u32[]{:S(2)}, u32[]{:S(2)}) collective-permute-start(f32[152,128]{1,0:T(8,128)} %shard_map.87.a_ref), channel_id=1, source_target_pairs={{0,16},{1,65},{2,18},{3,67},{4,20},{5,69},{6,22},{7,71},{8,24},{9,... | collective-permute-start | bytes 233480 | tf_op jit(solution)/shard_map/ppermute | solution.py:432
  3.8 6.1 %collective-permute-start.1 = (f32[152,128]{1,0:T(8,128)}, f32[152,128]{1,0:T(8,128)S(1)}, u32[]{:S(2)}, u32[]{:S(2)}) collective-permute-start(f32[152,128]{1,0:T(8,128)} %shard_map.87.a_ref), channel_id=1, source_target_pairs={{0,32},{1,129},{2,34},{3,131},{4,36},{5,133},{6,38},{7,135},{8,40}... | collective-permute-start | bytes 233480 | tf_op jit(solution)/shard_map/ppermute | solution.py:432
  4.5 5.6 %collective-permute-start.2 = (f32[152,128]{1,0:T(8,128)}, f32[152,128]{1,0:T(8,128)S(1)}, u32[]{:S(2)}, u32[]{:S(2)}) collective-permute-start(f32[152,128]{1,0:T(8,128)} %shard_map.87.a_ref), channel_id=1, source_target_pairs={{0,48},{1,193},{2,50},{3,195},{4,52},{5,197},{6,54},{7,199},{8,56}... | collective-permute-start | bytes 233480 | tf_op jit(solution)/shard_map/ppermute | solution.py:432
  6.3 0.7 copy-start.2
  10.1 0.9 copy-start.1
  11.0 9.1 %collective-permute-start.3 = (f32[4,152,128]{2,1,0:T(8,128)S(1)}, f32[4,152,128]{2,1,0:T(8,128)S(1)}, u32[]{:S(2)}, u32[]{:S(2)}) collective-permute-start(f32[4,152,128]{2,1,0:T(8,128)S(1)} %shard_map.88.w0), channel_id=1, source_target_pairs={{1,17},{2,66},{3,19},{4,68},{6,70},{9,25},{12,76},{15,31},{17,33},... | collective-permute-start | bytes 933896 | tf_op jit(solution)/shard_map/ppermute | solution.py:432
  14.1 7.7 %collective-permute-start.4 = (f32[4,152,128]{2,1,0:T(8,128)S(1)}, f32[4,152,128]{2,1,0:T(8,128)S(1)}, u32[]{:S(2)}, u32[]{:S(2)}) collective-permute-start(f32[4,152,128]{2,1,0:T(8,128)S(1)} %shard_map.88.w0), channel_id=1, source_target_pairs={{0,128},{1,33},{3,35},{6,134},{8,136},{10,138},{17,49},{19,51},{21... | collective-permute-start | bytes 933896 | tf_op jit(solution)/shard_map/ppermute | solution.py:432
  15.4 6.4 %collective-permute-start.5 = (f32[4,152,128]{2,1,0:T(8,128)S(1)}, f32[4,152,128]{2,1,0:T(8,128)S(1)}, u32[]{:S(2)}, u32[]{:S(2)}) collective-permute-start(f32[4,152,128]{2,1,0:T(8,128)S(1)} %shard_map.88.w0), channel_id=1, source_target_pairs={{1,49},{3,51},{4,196},{5,53},{10,202},{11,59},{12,204},{14,206},{1... | collective-permute-start | bytes 933896 | tf_op jit(solution)/shard_map/ppermute | solution.py:432
  22.6 2.1 copy-start.3
  22.6 1.3 collective-permute-start.6
  23.9 1.3 collective-permute-start.7
  24.1 1.2 collective-permute-start.8
  24.5 1.2 collective-permute-start.9
  25.7 1.4 collective-permute-start.10
  26.2 182.7 %copy-start.4 = (f32[288]{0:T(512)S(1)}, f32[288]{0:T(512)}, u32[]{:S(2)}) copy-start(f32[288]{0:T(512)} %potential_ref.1) | copy-start | bytes 3460
  28.6 180.2 %all-to-all-start = ((f32[16,1,288]{2,1,0:T(1,128)}), f32[16,1,288]{2,1,0:T(1,128)S(1)}, u32[]{:S(2)}, u32[]{:S(2)}) async-start(f32[16,1,288]{2,1,0:T(1,128)} %all_to_all.11), calls=%async_computation | async-start | bytes 49152 | tf_op jit(solution)/shard_map/all_to_all | solution.py:571
  175.0 35.3 %collective-permute-start.11 = (f32[36,128]{1,0:T(8,128)S(1)}, f32[36,128]{1,0:T(8,128)S(1)}, u32[]{:S(2)}, u32[]{:S(2)}) collective-permute-start(f32[36,128]{1,0:T(8,128)S(1)} %broadcast_select_fusion), channel_id=1, source_target_pairs={{0,5},{1,6},{2,10},{3,12},{4,13},{5,0},{6,1},{7,14},{8,11},{9,15},... | collective-permute-start | bytes 55304 | tf_op jit(solution)/shard_map/ppermute | solution.py:432

commit v2 on v1

--- a/solution.py
+++ b/solution.py
@@ -135,7 +135,9 @@
         weights_ref[s, 192:256, :] = extra_rows(bias + moved)
 
 
-def plan_work(count_ref, local_ref, plan_ref):
+def plan_work(count_ref, local_ref, wire_ref, plan_ref, near_wire_ref, sem):
+    copy = pltpu.make_async_copy(wire_ref, near_wire_ref, sem)
+    copy.start()
     src_tiles = local_ref.shape[0] - 6
     per_tile = 256 // unit_rows
     units = count_ref.shape[0] * per_tile
@@ -179,6 +181,7 @@
     plan_ref[src_tiles + 1 : src_tiles + 2, :] = items[0]
     plan_ref[src_tiles + 2 : src_tiles + 3, :] = items[1]
     plan_ref[src_tiles + 3 : src_tiles + 4, :] = begin
+    copy.wait()
 
 
 def pipeline(plan_ref, items, operand_ref, weights_ref, buffers, visit):
@@ -209,11 +212,25 @@
     lax.fori_loop(0, (items + span - 1) // span, step, 0)
 
 
+def distance():
+    row = lax.axis_index("row")
+    return lax.rem(lax.axis_index("col") - row + 2 - lax.rem(row, 2) + 16, 16)
+
+
 def on_duty(which):
-    row = lax.axis_index("row")
-    apart = lax.axis_index("col") - row + 2 - lax.rem(row, 2) + 16
-    near = lax.rem(apart, 16) < 4
+    near = distance() < 4
     return near if which == 0 else jnp.logical_not(near)
+
+
+def finish_sources(known_ref, rest_ref, mass_ref, live_ref, out_ref):
+    apart = distance()
+    odd = lax.rem(lax.axis_index("row"), 2) == 1
+    here = (apart < 4) | (apart == 5) | (apart == 6)
+    here |= (apart == jnp.where(odd, 15, 4)) | (apart == jnp.where(odd, 9, 10))
+    total = jnp.where(here, known_ref[...], rest_ref[...])
+    out_ref[...] = jnp.where(
+        live_ref[...] > 0.0, (entropy * ln2) * (mass_ref[...] - total), 0.0
+    )
 
 
 def row_pass(
@@ -458,23 +475,27 @@
     def second_hop(r, c, k):
         return around(r, k, 0) if c % 2 == 0 else around(r, 0, k)
 
+    slot_on = jnp.arange(slots, dtype=jnp.int32)[None, :] < partner_count[:, None]
+    local = jnp.where(slot_on, partners - col_here * dst_tiles, -1)
+    plan, near_wire = pl.pallas_call(
+        plan_work,
+        out_shape=(
+            jax.ShapeDtypeStruct((24, 128), jnp.int32),
+            jax.ShapeDtypeStruct(wire.shape, f32),
+        ),
+        in_specs=[smem, vmem, anywhere],
+        out_specs=(vmem, vmem),
+        scratch_shapes=[pltpu.SemaphoreType.DMA],
+        compiler_params=params,
+    )(dst_count, jnp.pad(local, ((0, 24 - src_tiles), (0, 0)), constant_values=-1), wire)
     bundle = pl.pallas_call(
         join,
         out_shape=jax.ShapeDtypeStruct((ring,) + wire.shape, f32),
         in_specs=[vmem] * ring,
         out_specs=vmem,
         compiler_params=params,
-    )(wire, *[send(wire, [((r, c), (first_hop(r, c, k), c)) for r, c in every]) for k in (1, 2, 3)])
+    )(near_wire, *[send(wire, [((r, c), (first_hop(r, c, k), c)) for r, c in every]) for k in (1, 2, 3)])
     busy = [set(near[r] + far[r][:2]) for r in range(rows)]
-    slot_on = jnp.arange(slots, dtype=jnp.int32)[None, :] < partner_count[:, None]
-    local = jnp.where(slot_on, partners - col_here * dst_tiles, -1)
-    plan = pl.pallas_call(
-        plan_work,
-        out_shape=jax.ShapeDtypeStruct((24, 128), jnp.int32),
-        in_specs=[smem, vmem],
-        out_specs=vmem,
-        compiler_params=params,
-    )(dst_count, jnp.pad(local, ((0, 24 - src_tiles), (0, 0)), constant_values=-1))
     plan, local, dst_count, src_count, bundle = lax.optimization_barrier(
         (plan, local, dst_count, src_count, bundle)
     )
@@ -542,7 +563,13 @@
     loops = [
         [(r, c) for c in (far[r][k], near[r][k], far[r][k] ^ 1)] for r in range(rows) for k in (0, 1)
     ]
-    early = send(far_lse, [(loop[i], loop[(i + 1) % 3]) for loop in loops for i in range(3)])
+    hops = [(loop[i], loop[(i + 1) % 3]) for loop in loops for i in range(3)]
+    for r in range(rows):
+        taken = near[r] + far[r][:2] + [c ^ 1 for c in far[r][:2]]
+        spare = [c for c in range(cols) if c not in taken][:2]
+        for a, c in zip(near[r][2:], spare):
+            hops += [((r, a), (r, c)), ((r, c), (r, a))]
+    early = send(far_lse, hops)
     near_lse = sum_rows(0, heavy)
     got_early = (col_here == row_here) | (col_here == row_here + 1 - 2 * parity)
     lse = log_sum([near_lse, jnp.where(got_early, early, nothing)])
@@ -570,12 +597,14 @@
     )
     shared_out = lax.all_to_all(col_part.reshape(rows, share), "row", 0, 0)
 
-    row_lse = jnp.where(in_near | in_far, known, rest)
-    src_potential = jnp.where(
-        half_live,
-        entropy * (-jnp.log(counted)[:, None] - math.log(all_src) - ln2 * row_lse),
-        0.0,
-    ).reshape(-1)
+    src_potential = pl.pallas_call(
+        finish_sources,
+        out_shape=jax.ShapeDtypeStruct((halves, tile // 2), f32),
+        in_specs=[vmem] * 4,
+        out_specs=vmem,
+        compiler_params=params,
+        cost_estimate=heavy,
+    )(known, rest, mass, half_live.astype(f32)).reshape(-1)
 
     spot = row_here * share + jnp.arange(share, dtype=jnp.int32)
     spot_tile = spot // tile

time: 211 us -> 213 us (level)
  the two profiles are of different devices: /device:TPU:20 before, /device:TPU:88 now
where the time goes in v2:
time: 213 us; the launch traced here: 214 us
  Pallas kernels  131 us (62%)
  starting transfers between devices  64.6 us (30%)
  waiting for transfers between devices  10.3 us (5%)
  local copies, waits for them, and re-layouts  4.26 us (2%)
  other arithmetic  3.65 us (2%)
    pallas_call x2, Pallas kernels, sum_columns(): pl.pallas_call(functools.partial(column_pass, which), out_shape=jax.Shape...  66.3 us
    pallas_call x2, Pallas kernels, sum_rows(): pl.pallas_call(functools.partial(row_pass, which), out_shape=jax.ShapeDty...  60.4 us
    ppermute x12, starting transfers between devices, send(): lax.ppermute(a, ('row', 'col'), filled(hops, rows * cols, cols) if full e...  53.4 us
    all_to_all x1, starting transfers between devices, shards(): shared_out = lax.all_to_all(col_part.reshape(rows, share), 'row', 0, 0)  11.2 us
    ppermute x12, waiting for transfers between devices, send(): lax.ppermute(a, ('row', 'col'), filled(hops, rows * cols, cols) if full e...  10.3 us
  transfers between devices with their start and end apart: 13, of which 4 were waited for; matrix products, arithmetic and copies ran while one was open for 3% of the time, Pallas kernels for 60%

profile of v2, /device:TPU:88, one launch (start us, length us, event | category | flops | bytes accessed | tf_op | source)
XLA Modules:
  0.0 214.3 jit_solution(12466805505514573824)
XLA Ops:
  0.6 0.0 copy-start
  0.6 1.8 shard_map.86.wire_ref
  2.5 0.3 collective-permute-start
  2.8 2.6 %collective-permute-start.1 = (f32[152,128]{1,0:T(8,128)}, f32[152,128]{1,0:T(8,128)S(1)}, u32[]{:S(2)}, u32[]{:S(2)}) collective-permute-start(f32[152,128]{1,0:T(8,128)} %shard_map.86.wire_ref), channel_id=1, source_target_pairs={{0,32},{1,129},{2,34},{3,131},{4,36},{5,133},{6,38},{7,135},{8,40}... | collective-permute-start | bytes 233480 | tf_op jit(solution)/shard_map/ppermute | solution.py:449
  5.4 0.0 collective-permute-start.2
  5.4 0.8 subtract_select_fusion
  6.2 0.0 copy-start.1
  6.2 0.9 copy-done.1
  7.1 0.0 copy-start.2
  7.1 0.7 copy-done.2
  7.7 1.5 shard_map.87
  9.3 0.0 collective-permute-done.b_ref
  9.3 0.0 collective-permute-done.1.c_ref
  9.3 1.8 collective-permute-done.2.d_ref
  11.2 1.3 collective-permute-start.3
  12.5 1.3 collective-permute-start.4
  13.8 1.3 collective-permute-start.5
  15.1 0.7 broadcast_in_dim.78
  15.8 0.1 lt.87
  15.9 0.5 fusion
  16.4 0.7 fusion.6.need_ref
  17.1 0.1 fusion.7.live_ref
  17.2 0.7 negate_add_fusion
  17.9 0.1 broadcast_in_dim.79
  17.9 0.1 sub.75
  18.0 0.7 lt.82
  18.8 0.1 lt.83
  18.9 0.1 and.55
  18.9 0.1 and.56
  19.0 0.1 fusion.8
  19.1 5.4 %collective-permute-done.3.w1 = f32[4,152,128]{2,1,0:T(8,128)S(1)} collective-permute-done((f32[4,152,128]{2,1,0:T(8,128)S(1)}, f32[4,152,128]{2,1,0:T(8,128)S(1)}, u32[]{:S(2)}, u32[]{:S(2)}) %collective-permute-start.3) | collective-permute-done | bytes 311328 | tf_op jit(solution)/shard_map/ppermute | solution.py:449
  24.5 0.0 collective-permute-done.4.w2
  24.6 0.0 collective-permute-done.5.w3
  24.6 0.0 copy-done
  24.6 0.0 copy-start.3
  24.6 0.1 collective-permute-start.6
  24.7 60.3 %shard_map.89 = f32[36,128]{1,0:T(8,128)S(1)} custom-call(s32[24,128]{1,0:T(8,128)S(1)} %get-tuple-element.12.sheet_ref, f32[64,4608]{1,0:T(8,128)S(1)} %bitcast.12, f32[18,256]{1,0:T(8,128)S(1)} %fusion.6.need_ref, f32[4,152,128]{2,1,0:T(8,128)S(1)} %shard_map.88.w0, f32[4,152,128]{2,1,0:T(8,128)S(1)} %collective-permute-done.3.w1, ...), custom_call_target="tpu_custom_call" | custom-call | flops 8000000000 | bytes 4000000 | tf_op jit(solution)/shard_map/pallas_call | solution.py:541
  85.0 0.0 collective-permute-done.6
  85.1 0.1 collective-permute-start.7
  85.2 0.1 collective-permute-start.8
  85.3 1.8 collective-permute-start.9
  87.1 0.0 copy-done.3
  87.1 0.1 select_reduce_fusion
  87.2 0.0 collective-permute-done.7
  87.2 1.9 collective-permute-done.8
  89.1 0.0 collective-permute-done.9
  89.1 0.3 collective-permute-start.10
  89.4 66.3 %shard_map.91.other_ref = f32[36,128]{1,0:T(8,128)S(1)} custom-call(s32[24,128]{1,0:T(8,128)S(1)} %get-tuple-element.12.sheet_ref, f32[64,4608]{1,0:T(8,128)S(1)} %bitcast.13, f32[36,128]{1,0:T(8,128)S(1)} %get-tuple-element.21.need_ref, f32[4,152,128]{2,1,0:T(8,128)S(1)} %shard_map.88.w0, f32[4,152,128]{2,1,0:T(8,128)S(1)} %collective-permute-done.3.w1, ...), custom_call_target="tpu_custom_call" | custom-call | flops 8000000000 | bytes 4000000 | tf_op jit(solution)/shard_map/pallas_call | solution.py:552
  155.7 0.0 copy-start.4
  155.7 0.0 collective-permute-done.10.lse_ref
  155.7 0.7 all_to_all.11
  156.4 11.2 %all-to-all-start = ((f32[16,1,288]{2,1,0:T(1,128)}), f32[16,1,288]{2,1,0:T(1,128)S(1)}, u32[]{:S(2)}, u32[]{:S(2)}) async-start(f32[16,1,288]{2,1,0:T(1,128)} %all_to_all.11), calls=%async_computation | async-start | bytes 49152 | tf_op jit(solution)/shard_map/all_to_all | solution.py:598
  167.6 44.3 %collective-permute-start.11 = (f32[36,128]{1,0:T(8,128)S(1)}, f32[36,128]{1,0:T(8,128)S(1)}, u32[]{:S(2)}, u32[]{:S(2)}) collective-permute-start(f32[36,128]{1,0:T(8,128)S(1)} %broadcast_select_fusion.known_ref), channel_id=1, source_target_pairs={{0,5},{1,6},{2,10},{3,12},{4,13},{5,0},{6,1},{7,14},{8,11},{9,15},... | collective-permute-start | bytes 55304 | tf_op jit(solution)/shard_map/ppermute | solution.py:449
  211.9 0.0 all-to-all-done
  212.0 0.0 copy-done.4
  212.0 0.6 add_select_fusion.1
  212.6 1.1 collective-permute-done.11.rest_ref
  213.7 0.6 shard_map.92
  (17 shorter events, 0.3 us)
Async XLA Ops:
  0.6 23.9 %copy-start = (f32[4608,64]{0,1:T(8,128)S(1)}, f32[4608,64]{0,1:T(8,128)}, u32[]{:S(2)}) copy-start(f32[4608,64]{0,1:T(8,128)} %param.7) | copy-start | bytes 3538948
  2.5 6.8 %collective-permute-start = (f32[152,128]{1,0:T(8,128)}, f32[152,128]{1,0:T(8,128)S(1)}, u32[]{:S(2)}, u32[]{:S(2)}) collective-permute-start(f32[152,128]{1,0:T(8,128)} %shard_map.86.wire_ref), channel_id=1, source_target_pairs={{0,16},{1,65},{2,18},{3,67},{4,20},{5,69},{6,22},{7,71},{8,24},{9,... | collective-permute-start | bytes 233480 | tf_op jit(solution)/shard_map/ppermute | solution.py:449
  2.8 6.6 %collective-permute-start.1 = (f32[152,128]{1,0:T(8,128)}, f32[152,128]{1,0:T(8,128)S(1)}, u32[]{:S(2)}, u32[]{:S(2)}) collective-permute-start(f32[152,128]{1,0:T(8,128)} %shard_map.86.wire_ref), channel_id=1, source_target_pairs={{0,32},{1,129},{2,34},{3,131},{4,36},{5,133},{6,38},{7,135},{8,40}... | collective-permute-start | bytes 233480 | tf_op jit(solution)/shard_map/ppermute | solution.py:449
  5.4 5.8 %collective-permute-start.2 = (f32[152,128]{1,0:T(8,128)}, f32[152,128]{1,0:T(8,128)S(1)}, u32[]{:S(2)}, u32[]{:S(2)}) collective-permute-start(f32[152,128]{1,0:T(8,128)} %shard_map.86.wire_ref), channel_id=1, source_target_pairs={{0,48},{1,193},{2,50},{3,195},{4,52},{5,197},{6,54},{7,199},{8,56}... | collective-permute-start | bytes 233480 | tf_op jit(solution)/shard_map/ppermute | solution.py:449
  6.2 0.9 copy-start.1
  7.1 0.7 copy-start.2
  11.2 13.3 %collective-permute-start.3 = (f32[4,152,128]{2,1,0:T(8,128)S(1)}, f32[4,152,128]{2,1,0:T(8,128)S(1)}, u32[]{:S(2)}, u32[]{:S(2)}) collective-permute-start(f32[4,152,128]{2,1,0:T(8,128)S(1)} %shard_map.88.w0), channel_id=1, source_target_pairs={{1,17},{2,66},{3,19},{4,68},{6,70},{9,25},{12,76},{15,31},{17,33},... | collective-permute-start | bytes 933896 | tf_op jit(solution)/shard_map/ppermute | solution.py:449
  12.5 12.0 %collective-permute-start.4 = (f32[4,152,128]{2,1,0:T(8,128)S(1)}, f32[4,152,128]{2,1,0:T(8,128)S(1)}, u32[]{:S(2)}, u32[]{:S(2)}) collective-permute-start(f32[4,152,128]{2,1,0:T(8,128)S(1)} %shard_map.88.w0), channel_id=1, source_target_pairs={{0,128},{1,33},{3,35},{6,134},{8,136},{10,138},{17,49},{19,51},{21... | collective-permute-start | bytes 933896 | tf_op jit(solution)/shard_map/ppermute | solution.py:449
  13.8 10.7 %collective-permute-start.5 = (f32[4,152,128]{2,1,0:T(8,128)S(1)}, f32[4,152,128]{2,1,0:T(8,128)S(1)}, u32[]{:S(2)}, u32[]{:S(2)}) collective-permute-start(f32[4,152,128]{2,1,0:T(8,128)S(1)} %shard_map.88.w0), channel_id=1, source_target_pairs={{1,49},{3,51},{4,196},{5,53},{10,202},{11,59},{12,204},{14,206},{1... | collective-permute-start | bytes 933896 | tf_op jit(solution)/shard_map/ppermute | solution.py:449
  24.6 62.5 %copy-start.3 = (s32[18]{0:T(128)S(1)}, s32[18]{0:T(128)}, u32[]{:S(2)}) copy-start(s32[18]{0:T(128)} %count_ref.3) | copy-start | bytes 220
  24.6 60.4 %collective-permute-start.6 = (f32[36,128]{1,0:T(8,128)S(1)}, f32[36,128]{1,0:T(8,128)S(1)}, u32[]{:S(2)}, u32[]{:S(2)}) collective-permute-start(f32[36,128]{1,0:T(8,128)S(1)} %shard_map.90), channel_id=1, source_target_pairs={{0,3},{1,9},{2,0},{3,2},{4,14},{5,15},{6,7},{7,6},{8,1},{9,8},{10,... | collective-permute-start | bytes 55304 | tf_op jit(solution)/shard_map/ppermute | solution.py:449
  85.1 2.1 collective-permute-start.7
  85.2 3.9 %collective-permute-start.8 = (f32[36,128]{1,0:T(8,128)S(1)}, f32[36,128]{1,0:T(8,128)S(1)}, u32[]{:S(2)}, u32[]{:S(2)}) collective-permute-start(f32[36,128]{1,0:T(8,128)S(1)} %multiply_add_fusion.1), channel_id=1, source_target_pairs={{0,14},{1,15},{2,3},{3,2},{4,5},{5,4},{6,7},{7,6},{8,9},{9,8},{10,... | collective-permute-start | bytes 55304 | tf_op jit(solution)/shard_map/ppermute | solution.py:449
  85.3 3.8 %collective-permute-start.9 = (f32[36,128]{1,0:T(8,128)S(1)}, f32[36,128]{1,0:T(8,128)S(1)}, u32[]{:S(2)}, u32[]{:S(2)}) collective-permute-start(f32[36,128]{1,0:T(8,128)S(1)} %multiply_add_fusion.1), channel_id=1, source_target_pairs={{0,15},{1,14},{2,3},{3,2},{4,5},{5,4},{6,7},{7,6},{8,9},{9,8},{10,... | collective-permute-start | bytes 55304 | tf_op jit(solution)/shard_map/ppermute | solution.py:449
  89.1 66.6 %collective-permute-start.10 = (f32[36,128]{1,0:T(8,128)S(1)}, f32[36,128]{1,0:T(8,128)S(1)}, u32[]{:S(2)}, u32[]{:S(2)}) collective-permute-start(f32[36,128]{1,0:T(8,128)S(1)} %multiply_add_fusion.lse_ref), channel_id=1, source_target_pairs={{0,2},{1,8},{2,0},{3,14},{4,15},{5,9},{6,7},{7,6},{8,1},{9,5},{10,... | collective-permute-start | bytes 55304 | tf_op jit(solution)/shard_map/ppermute | solution.py:449
  155.7 56.3 %copy-start.4 = (f32[288]{0:T(512)S(1)}, f32[288]{0:T(512)}, u32[]{:S(2)}) copy-start(f32[288]{0:T(512)} %potential_ref.1) | copy-start | bytes 3460
  156.4 55.5 %all-to-all-start = ((f32[16,1,288]{2,1,0:T(1,128)}), f32[16,1,288]{2,1,0:T(1,128)S(1)}, u32[]{:S(2)}, u32[]{:S(2)}) async-start(f32[16,1,288]{2,1,0:T(1,128)} %all_to_all.11), calls=%async_computation | async-start | bytes 49152 | tf_op jit(solution)/shard_map/all_to_all | solution.py:598
  167.6 46.1 %collective-permute-start.11 = (f32[36,128]{1,0:T(8,128)S(1)}, f32[36,128]{1,0:T(8,128)S(1)}, u32[]{:S(2)}, u32[]{:S(2)}) collective-permute-start(f32[36,128]{1,0:T(8,128)S(1)} %broadcast_select_fusion.known_ref), channel_id=1, source_target_pairs={{0,5},{1,6},{2,10},{3,12},{4,13},{5,0},{6,1},{7,14},{8,11},{9,15},... | collective-permute-start | bytes 55304 | tf_op jit(solution)/shard_map/ppermute | solution.py:449

commit v3 on v2

--- a/solution.py
+++ b/solution.py
@@ -321,15 +321,24 @@
         )
 
         def to_row(column):
-            return jnp.sum(jnp.where(eye, column, 0.0), axis=0, keepdims=True)
-
+            return jnp.sum(
+                jnp.where(eye[0 : column.shape[0]], column, 0.0), axis=0, keepdims=True
+            )
+
+        blocks = [
+            (shard, slice(128 * i, 128 * i + size), slice(shard * 288 + 128 * i, shard * 288 + 128 * i + size))
+            for shard in range(out_ref.shape[0])
+            for i, size in enumerate((128, 128, 32))
+        ]
         bad = jnp.zeros((1, 128), f32)
-        for u in range(out_ref.shape[0]):
-            sums = to_row(jnp.sum(total_ref[u * 128 : (u + 1) * 128, :], axis=1, keepdims=True))
-            out_ref[u : u + 1, :] = jnp.where(
+        for shard, lanes, where in blocks:
+            sums = to_row(jnp.sum(total_ref[where, :], axis=1, keepdims=True))
+            size = lanes.stop - lanes.start
+            out_ref[shard, :, lanes] = jnp.where(
                 sums > 0.0, jnp.log2(jnp.maximum(sums, 1e-37)), nothing
-            )
-            bad = jnp.maximum(bad, jnp.where(sums > 1e-25, 0.0, need_ref[u : u + 1, :]))
+            )[:, 0:size]
+            needed = need_ref[3 * shard + lanes.start // 128 : 3 * shard + lanes.start // 128 + 1, :]
+            bad = jnp.maximum(bad, jnp.where(sums > 1e-25, 0.0, needed))
 
         @pl.when(jnp.max(bad) > 0.0)
         def _():
@@ -359,18 +368,15 @@
 
             lax.fori_loop(0, tiles, one_tile, 0)
 
-            def finish(u, carry):
-                where = pl.ds(pl.multiple_of(u * 128, 128), 128)
+            for shard, lanes, where in blocks:
                 high = high_ref[where, :]
                 top = jnp.max(high, axis=1, keepdims=True)
                 rest = total_ref[where, :] * jnp.exp2(high - top)
                 sums = to_row(jnp.sum(rest, axis=1, keepdims=True))
-                out_ref[pl.ds(u, 1), :] = jnp.where(
+                size = lanes.stop - lanes.start
+                out_ref[shard, :, lanes] = jnp.where(
                     sums > 0.0, to_row(top) + jnp.log2(jnp.maximum(sums, 1e-37)), nothing
-                )
-                return carry
-
-            lax.fori_loop(0, out_ref.shape[0], finish, 0)
+                )[:, 0:size]
 
     @pl.when(on_duty(which))
     def _():
@@ -517,7 +523,8 @@
     wanted = jnp.any(local[:, :, None] == jnp.arange(dst_tiles, dtype=jnp.int32), axis=1)
     src_need = jnp.where(src_live & jnp.any(wanted, axis=1)[:, None], 1.0, 0.0)
     dst_need = jnp.where(dst_live & jnp.any(wanted, axis=0)[:, None], 1.0, 0.0)
-    dst_need = dst_need.reshape(points // 128, 128)
+    dst_need = jnp.pad(dst_need.reshape(rows, share), ((0, 0), (0, 384 - share)))
+    dst_need = dst_need.reshape(rows * 3, 128)
     counted = jnp.repeat(src_count.astype(f32), 2)
     half_live = (place[:128][None, :] + 128 * (jnp.arange(2 * src_tiles) % 2)[:, None]) < jnp.repeat(
         src_count, 2
@@ -551,7 +558,7 @@
     def sum_columns(which, lse, other, cost):
         return pl.pallas_call(
             functools.partial(column_pass, which),
-            out_shape=jax.ShapeDtypeStruct((points // 128, 128), f32),
+            out_shape=jax.ShapeDtypeStruct((rows, 1, share), f32),
             in_specs=[anywhere] + [vmem] * (5 + ring),
             out_specs=vmem,
             scratch_shapes=scratch + [pltpu.VMEM((points + unit_rows, 128), f32)] * 2 + buffers,
@@ -586,7 +593,7 @@
         ]
     )
     spread = send(lse, [((r, near[r][k]), (r, far[r][k])) for r in range(rows) for k in range(4)])
-    blank = jnp.full((points // 128, 128), nothing, f32)
+    blank = jnp.full((rows, 1, share), nothing, f32)
     near_part = sum_columns(0, lse, blank, heavy)
     col_part = sum_columns(1, spread, near_part, light)
     known = jnp.where(in_far, spread, lse)
@@ -595,7 +602,7 @@
         known,
         [((r, (near[r] + far[r])[k]), (r, far[r][4 + k])) for r in range(rows) for k in range(8)],
     )
-    shared_out = lax.all_to_all(col_part.reshape(rows, share), "row", 0, 0)
+    shared_out = lax.all_to_all(col_part, "row", 0, 0)[:, 0]
 
     src_potential = pl.pallas_call(
         finish_sources,
@@ -606,6 +613,7 @@
         cost_estimate=heavy,
     )(known, rest, mass, half_live.astype(f32)).reshape(-1)
 
+    src_potential, dst_potential = lax.optimization_barrier((src_potential, dst_potential))
     spot = row_here * share + jnp.arange(share, dtype=jnp.int32)
     spot_tile = spot // tile
     spot_count = jnp.sum(

time: 213 us -> 224 us (1.052)
  the two profiles are of different devices: /device:TPU:88 before, /device:TPU:75 now
where the time goes in v3:
time: 224 us; the launch traced here: 227 us
  Pallas kernels  130 us (58%)
  starting transfers between devices  83.8 us (37%)
  waiting for transfers between devices  5.36 us (2%)
  other arithmetic  4.36 us (2%)
  local copies, waits for them, and re-layouts  2.64 us (1%)
    ppermute x12, starting transfers between devices, send(): lax.ppermute(a, ('row', 'col'), filled(hops, rows * cols, cols) if full e...  73.2 us
    pallas_call x2, Pallas kernels, sum_columns(): pl.pallas_call(functools.partial(column_pass, which), out_shape=jax.Shape...  64.8 us
    pallas_call x2, Pallas kernels, sum_rows(): pl.pallas_call(functools.partial(row_pass, which), out_shape=jax.ShapeDty...  61.1 us
    all_to_all x1, starting transfers between devices, shards(): shared_out = lax.all_to_all(col_part, 'row', 0, 0)[:, 0]  10.5 us
    ppermute x12, waiting for transfers between devices, send(): lax.ppermute(a, ('row', 'col'), filled(hops, rows * cols, cols) if full e...  5.36 us
  transfers between devices with their start and end apart: 13, of which 4 were waited for; matrix products, arithmetic and copies ran while one was open for 2% of the time, Pallas kernels for 56%

profile of v3, /device:TPU:75, one launch (start us, length us, event | category | flops | bytes accessed | tf_op | source)
XLA Modules:
  0.0 227.0 jit_solution(11244096821895217993)
XLA Ops:
  0.6 0.0 copy-start
  0.6 1.8 shard_map.86.wire_ref
  2.5 1.3 collective-permute-start
  3.8 0.8 collective-permute-start.1
  4.6 1.9 collective-permute-start.2
  6.5 0.8 subtract_select_fusion
  7.3 0.0 copy-start.1
  7.3 0.9 copy-done.1
  8.2 0.0 copy-start.2
  8.2 0.7 copy-done.2
  8.8 1.5 shard_map.87
  10.4 0.0 collective-permute-done.b_ref
  10.4 0.0 collective-permute-done.1.c_ref
  10.4 0.0 collective-permute-done.2.d_ref
  10.5 3.2 %collective-permute-start.3 = (f32[4,152,128]{2,1,0:T(8,128)S(1)}, f32[4,152,128]{2,1,0:T(8,128)S(1)}, u32[]{:S(2)}, u32[]{:S(2)}) collective-permute-start(f32[4,152,128]{2,1,0:T(8,128)S(1)} %shard_map.88.w0), channel_id=1, source_target_pairs={{1,17},{2,66},{3,19},{4,68},{6,70},{9,25},{12,76},{15,31},{17,33},... | collective-permute-start | bytes 933896 | tf_op jit(solution)/shard_map/ppermute | solution.py:455
  13.7 2.6 %collective-permute-start.4 = (f32[4,152,128]{2,1,0:T(8,128)S(1)}, f32[4,152,128]{2,1,0:T(8,128)S(1)}, u32[]{:S(2)}, u32[]{:S(2)}) collective-permute-start(f32[4,152,128]{2,1,0:T(8,128)S(1)} %shard_map.88.w0), channel_id=1, source_target_pairs={{0,128},{1,33},{3,35},{6,134},{8,136},{10,138},{17,49},{19,51},{21... | collective-permute-start | bytes 933896 | tf_op jit(solution)/shard_map/ppermute | solution.py:455
  16.3 4.0 %collective-permute-start.5 = (f32[4,152,128]{2,1,0:T(8,128)S(1)}, f32[4,152,128]{2,1,0:T(8,128)S(1)}, u32[]{:S(2)}, u32[]{:S(2)}) collective-permute-start(f32[4,152,128]{2,1,0:T(8,128)S(1)} %shard_map.88.w0), channel_id=1, source_target_pairs={{1,49},{3,51},{4,196},{5,53},{10,202},{11,59},{12,204},{14,206},{1... | collective-permute-start | bytes 933896 | tf_op jit(solution)/shard_map/ppermute | solution.py:455
  20.3 0.5 fusion
  20.8 0.7 negate_add_fusion
  21.4 0.7 fusion.6.need_ref
  22.2 0.7 broadcast_in_dim.74
  22.9 0.1 lt.70
  23.0 0.1 broadcast_in_dim.75
  23.0 0.1 sub.75
  23.1 0.1 fusion.10.mass_ref
  23.2 0.1 fusion.9.live_ref
  23.3 0.7 fusion.8
  24.0 0.0 collective-permute-done.3.w1
  24.0 0.0 collective-permute-done.4.w2
  24.1 2.4 %collective-permute-done.5.w3 = f32[4,152,128]{2,1,0:T(8,128)S(1)} collective-permute-done((f32[4,152,128]{2,1,0:T(8,128)S(1)}, f32[4,152,128]{2,1,0:T(8,128)S(1)}, u32[]{:S(2)}, u32[]{:S(2)}) %collective-permute-start.5) | collective-permute-done | bytes 311328 | tf_op jit(solution)/shard_map/ppermute | solution.py:455
  26.5 0.0 copy-done
  26.5 0.0 copy-start.3
  26.5 0.1 collective-permute-start.6
  26.6 61.1 %shard_map.89 = f32[36,128]{1,0:T(8,128)S(1)} custom-call(s32[24,128]{1,0:T(8,128)S(1)} %get-tuple-element.14.sheet_ref, f32[64,4608]{1,0:T(8,128)S(1)} %bitcast.12, f32[18,256]{1,0:T(8,128)S(1)} %fusion.6.need_ref, f32[4,152,128]{2,1,0:T(8,128)S(1)} %shard_map.88.w0, f32[4,152,128]{2,1,0:T(8,128)S(1)} %collective-permute-done.3.w1, ...), custom_call_target="tpu_custom_call" | custom-call | flops 8000000000 | bytes 4000000 | tf_op jit(solution)/shard_map/pallas_call | solution.py:548
  87.6 0.0 collective-permute-done.6
  87.7 6.2 %collective-permute-start.7 = (f32[36,128]{1,0:T(8,128)S(1)}, f32[36,128]{1,0:T(8,128)S(1)}, u32[]{:S(2)}, u32[]{:S(2)}) collective-permute-start(f32[36,128]{1,0:T(8,128)S(1)} %multiply_add_fusion.1), channel_id=1, source_target_pairs={{0,1},{1,0},{2,3},{3,2},{4,5},{5,4},{6,7},{7,6},{8,9},{9,8},{10,11... | collective-permute-start | bytes 55304 | tf_op jit(solution)/shard_map/ppermute | solution.py:455
  93.9 0.0 collective-permute-start.8
  93.9 1.7 collective-permute-start.9
  95.6 0.0 copy-done.3
  95.6 0.1 select_reduce_fusion
  95.7 0.1 select_n.79
  95.8 0.0 collective-permute-done.7
  95.8 0.7 collective-permute-done.8
  96.5 0.8 collective-permute-done.9
  97.4 0.3 collective-permute-start.10
  97.7 64.2 %shard_map.91.other_ref = f32[16,1,288]{2,1,0:T(1,128)S(1)} custom-call(s32[24,128]{1,0:T(8,128)S(1)} %get-tuple-element.14.sheet_ref, f32[64,4608]{1,0:T(8,128)S(1)} %bitcast.13, f32[48,128]{1,0:T(8,128)S(1)} %reshape.76.need_ref, f32[4,152,128]{2,1,0:T(8,128)S(1)} %shard_map.88.w0, f32[4,152,128]{2,1,0:T(8,128)S(1)} %collective-permute-done.3.w1, ...), custom_call_target="tpu_custom_call" | custom-call | flops 8000000000 | bytes 4000000 | tf_op jit(solution)/shard_map/pallas_call | solution.py:559
  161.9 0.0 collective-permute-done.10.lse_ref
  161.9 0.7 shard_map.93
  162.5 10.5 %all-to-all-start = ((f32[16,1,288]{2,1,0:T(1,128)}), f32[16,1,288]{2,1,0:T(1,128)S(1)}, u32[]{:S(2)}, u32[]{:S(2)}) async-start(f32[16,1,288]{2,1,0:T(1,128)} %shard_map.93), calls=%async_computation | async-start | bytes 49152 | tf_op jit(solution)/shard_map/all_to_all | solution.py:605
  173.1 51.2 %collective-permute-start.11 = (f32[36,128]{1,0:T(8,128)S(1)}, f32[36,128]{1,0:T(8,128)S(1)}, u32[]{:S(2)}, u32[]{:S(2)}) collective-permute-start(f32[36,128]{1,0:T(8,128)S(1)} %broadcast_select_fusion.known_ref), channel_id=1, source_target_pairs={{0,5},{1,6},{2,10},{3,12},{4,13},{5,0},{6,1},{7,14},{8,11},{9,15},... | collective-permute-start | bytes 55304 | tf_op jit(solution)/shard_map/ppermute | solution.py:455
  224.3 0.0 all-to-all-done
  224.4 0.0 copy-start.4
  224.4 1.4 collective-permute-done.11.rest_ref
  225.8 0.6 shard_map.92
  226.4 0.0 copy-done.4
  226.4 0.6 add_select_fusion.1
  (15 shorter events, 0.2 us)
Async XLA Ops:
  0.6 25.8 %copy-start = (f32[4608,64]{0,1:T(8,128)S(1)}, f32[4608,64]{0,1:T(8,128)}, u32[]{:S(2)}) copy-start(f32[4608,64]{0,1:T(8,128)} %param.7) | copy-start | bytes 3538948
  2.5 7.9 %collective-permute-start = (f32[152,128]{1,0:T(8,128)}, f32[152,128]{1,0:T(8,128)S(1)}, u32[]{:S(2)}, u32[]{:S(2)}) collective-permute-start(f32[152,128]{1,0:T(8,128)} %shard_map.86.wire_ref), channel_id=1, source_target_pairs={{0,16},{1,65},{2,18},{3,67},{4,20},{5,69},{6,22},{7,71},{8,24},{9,... | collective-permute-start | bytes 233480 | tf_op jit(solution)/shard_map/ppermute | solution.py:455
  3.8 6.6 %collective-permute-start.1 = (f32[152,128]{1,0:T(8,128)}, f32[152,128]{1,0:T(8,128)S(1)}, u32[]{:S(2)}, u32[]{:S(2)}) collective-permute-start(f32[152,128]{1,0:T(8,128)} %shard_map.86.wire_ref), channel_id=1, source_target_pairs={{0,32},{1,129},{2,34},{3,131},{4,36},{5,133},{6,38},{7,135},{8,40}... | collective-permute-start | bytes 233480 | tf_op jit(solution)/shard_map/ppermute | solution.py:455
  4.6 5.8 %collective-permute-start.2 = (f32[152,128]{1,0:T(8,128)}, f32[152,128]{1,0:T(8,128)S(1)}, u32[]{:S(2)}, u32[]{:S(2)}) collective-permute-start(f32[152,128]{1,0:T(8,128)} %shard_map.86.wire_ref), channel_id=1, source_target_pairs={{0,48},{1,193},{2,50},{3,195},{4,52},{5,197},{6,54},{7,199},{8,56}... | collective-permute-start | bytes 233480 | tf_op jit(solution)/shard_map/ppermute | solution.py:455
  7.3 0.9 copy-start.1
  8.2 0.7 copy-start.2
  10.5 13.6 %collective-permute-start.3 = (f32[4,152,128]{2,1,0:T(8,128)S(1)}, f32[4,152,128]{2,1,0:T(8,128)S(1)}, u32[]{:S(2)}, u32[]{:S(2)}) collective-permute-start(f32[4,152,128]{2,1,0:T(8,128)S(1)} %shard_map.88.w0), channel_id=1, source_target_pairs={{1,17},{2,66},{3,19},{4,68},{6,70},{9,25},{12,76},{15,31},{17,33},... | collective-permute-start | bytes 933896 | tf_op jit(solution)/shard_map/ppermute | solution.py:455
  13.7 10.4 %collective-permute-start.4 = (f32[4,152,128]{2,1,0:T(8,128)S(1)}, f32[4,152,128]{2,1,0:T(8,128)S(1)}, u32[]{:S(2)}, u32[]{:S(2)}) collective-permute-start(f32[4,152,128]{2,1,0:T(8,128)S(1)} %shard_map.88.w0), channel_id=1, source_target_pairs={{0,128},{1,33},{3,35},{6,134},{8,136},{10,138},{17,49},{19,51},{21... | collective-permute-start | bytes 933896 | tf_op jit(solution)/shard_map/ppermute | solution.py:455
  16.3 10.1 %collective-permute-start.5 = (f32[4,152,128]{2,1,0:T(8,128)S(1)}, f32[4,152,128]{2,1,0:T(8,128)S(1)}, u32[]{:S(2)}, u32[]{:S(2)}) collective-permute-start(f32[4,152,128]{2,1,0:T(8,128)S(1)} %shard_map.88.w0), channel_id=1, source_target_pairs={{1,49},{3,51},{4,196},{5,53},{10,202},{11,59},{12,204},{14,206},{1... | collective-permute-start | bytes 933896 | tf_op jit(solution)/shard_map/ppermute | solution.py:455
  26.5 69.1 %copy-start.3 = (s32[18]{0:T(128)S(1)}, s32[18]{0:T(128)}, u32[]{:S(2)}) copy-start(s32[18]{0:T(128)} %count_ref.3) | copy-start | bytes 220
  26.5 61.2 %collective-permute-start.6 = (f32[36,128]{1,0:T(8,128)S(1)}, f32[36,128]{1,0:T(8,128)S(1)}, u32[]{:S(2)}, u32[]{:S(2)}) collective-permute-start(f32[36,128]{1,0:T(8,128)S(1)} %shard_map.90), channel_id=1, source_target_pairs={{0,3},{1,9},{2,0},{3,2},{4,14},{5,15},{6,7},{7,6},{8,1},{9,8},{10,... | collective-permute-start | bytes 55304 | tf_op jit(solution)/shard_map/ppermute | solution.py:455
  87.7 8.1 %collective-permute-start.7 = (f32[36,128]{1,0:T(8,128)S(1)}, f32[36,128]{1,0:T(8,128)S(1)}, u32[]{:S(2)}, u32[]{:S(2)}) collective-permute-start(f32[36,128]{1,0:T(8,128)S(1)} %multiply_add_fusion.1), channel_id=1, source_target_pairs={{0,1},{1,0},{2,3},{3,2},{4,5},{5,4},{6,7},{7,6},{8,9},{9,8},{10,11... | collective-permute-start | bytes 55304 | tf_op jit(solution)/shard_map/ppermute | solution.py:455
  93.9 2.7 %collective-permute-start.8 = (f32[36,128]{1,0:T(8,128)S(1)}, f32[36,128]{1,0:T(8,128)S(1)}, u32[]{:S(2)}, u32[]{:S(2)}) collective-permute-start(f32[36,128]{1,0:T(8,128)S(1)} %multiply_add_fusion.1), channel_id=1, source_target_pairs={{0,14},{1,15},{2,3},{3,2},{4,5},{5,4},{6,7},{7,6},{8,9},{9,8},{10,... | collective-permute-start | bytes 55304 | tf_op jit(solution)/shard_map/ppermute | solution.py:455
  93.9 3.5 %collective-permute-start.9 = (f32[36,128]{1,0:T(8,128)S(1)}, f32[36,128]{1,0:T(8,128)S(1)}, u32[]{:S(2)}, u32[]{:S(2)}) collective-permute-start(f32[36,128]{1,0:T(8,128)S(1)} %multiply_add_fusion.1), channel_id=1, source_target_pairs={{0,15},{1,14},{2,3},{3,2},{4,5},{5,4},{6,7},{7,6},{8,9},{9,8},{10,... | collective-permute-start | bytes 55304 | tf_op jit(solution)/shard_map/ppermute | solution.py:455
  97.4 64.5 %collective-permute-start.10 = (f32[36,128]{1,0:T(8,128)S(1)}, f32[36,128]{1,0:T(8,128)S(1)}, u32[]{:S(2)}, u32[]{:S(2)}) collective-permute-start(f32[36,128]{1,0:T(8,128)S(1)} %multiply_add_fusion.lse_ref), channel_id=1, source_target_pairs={{0,2},{1,8},{2,0},{3,14},{4,15},{5,9},{6,7},{7,6},{8,1},{9,5},{10,... | collective-permute-start | bytes 55304 | tf_op jit(solution)/shard_map/ppermute | solution.py:455
  162.5 61.8 %all-to-all-start = ((f32[16,1,288]{2,1,0:T(1,128)}), f32[16,1,288]{2,1,0:T(1,128)S(1)}, u32[]{:S(2)}, u32[]{:S(2)}) async-start(f32[16,1,288]{2,1,0:T(1,128)} %shard_map.93), calls=%async_computation | async-start | bytes 49152 | tf_op jit(solution)/shard_map/all_to_all | solution.py:605
  173.1 52.7 %collective-permute-start.11 = (f32[36,128]{1,0:T(8,128)S(1)}, f32[36,128]{1,0:T(8,128)S(1)}, u32[]{:S(2)}, u32[]{:S(2)}) collective-permute-start(f32[36,128]{1,0:T(8,128)S(1)} %broadcast_select_fusion.known_ref), channel_id=1, source_target_pairs={{0,5},{1,6},{2,10},{3,12},{4,13},{5,0},{6,1},{7,14},{8,11},{9,15},... | collective-permute-start | bytes 55304 | tf_op jit(solution)/shard_map/ppermute | solution.py:455
  224.4 2.0 copy-start.4
